TPU v7x, 512 devices: a whole 4x4x16 slice. The times are simulated.
512 devices in a mesh: seq: 32 (over x, y, core), tp: 16 (over z).
Axes of the slice: x: 4, y: 4, z: 16, core: 2. Of those that a mesh axis runs over, the one named last changes fastest.
Arguments:
- gate_values: bfloat16 [3072, 28672], P('seq', 'tp'), may hold values from -6 to 6
- up_values: bfloat16 [3072, 28672], P('seq', 'tp'), may hold values from -6 to 6
- weight_codes: bfloat16 [28672, 8192], P('tp', 'seq'), may hold values from -127 to 127
- exponents: int32 [8192], P('seq'), may hold values from -15 to -13
- token_scale: float32 [3072], replicated, may hold values from 0.006 to 0.06
Outputs:
- layer_output: bfloat16 [3072, 8192], P('tp', 'seq')
All inputs are finite; a program needn't handle non-finite values.
Results may differ from a plain program's by a relative error of at most 0.0048.
Values may be sent and summed in bfloat16 or wider, within the bound.
A program may use at most 64 MiB of HBM per device.

v0:
```python
import math

import jax
import jax.numpy as jnp
import numpy as np
from jax import lax
from jax.sharding import PartitionSpec as P


def from_partner(value, axis, stride):
    mask = 2**stride
    pairs = [(source, source ^ mask) for source in range(lax.axis_size(axis))]
    return lax.ppermute(value, axis, pairs)


def paley_table():
    residues = [number * number % 13 for number in range(1, 13)]
    legendre = np.array([0.0] + [1.0 if number in residues else -1.0 for number in range(1, 13)])
    offsets = (np.arange(13)[None, :] - np.arange(13)[:, None]) % 13
    conference = np.zeros((14, 14))
    conference[0, 1:] = 1.0
    conference[1:, 0] = 1.0
    conference[1:, 1:] = legendre[offsets]
    upper_pair = np.array([[1.0, 1.0], [1.0, -1.0]])
    lower_pair = np.array([[1.0, -1.0], [-1.0, -1.0]])
    paley_matrix = np.kron(conference, upper_pair) + np.kron(np.eye(14), lower_pair)
    return jnp.asarray(paley_matrix, dtype=jnp.float32)


def sylvester(matrix_order):
    table = np.ones((1, 1))
    doubling = np.array([[1.0, 1.0], [1.0, -1.0]])
    for level in range(matrix_order.bit_length() - 1):
        table = np.kron(doubling, table)
    return jnp.asarray(table, dtype=jnp.float32)


def scaled_product(row_piece, weight_codes, token_scale, column_scale):
    partial_rows = jnp.dot(row_piece, weight_codes, preferred_element_type=jnp.float32)
    return partial_rows * token_scale[:, None] * column_scale[None, :]


def body(gate_values, up_values, weight_codes, exponents, token_scale):
    tp_count = lax.axis_size("tp")
    tp_index = lax.axis_index("tp")
    seq_index = lax.axis_index("seq")
    row_count = gate_values.shape[0]
    shard_width = gate_values.shape[1]
    local_order = shard_width // 28
    hidden = jax.nn.silu(gate_values.astype(jnp.float32)) * up_values.astype(jnp.float32)
    blocked = hidden.reshape(row_count, local_order, 28)
    paley_mixed = jnp.einsum("tce,ae->tca", blocked, paley_table(), precision=lax.Precision.HIGHEST)
    local_mixed = jnp.einsum(
        "tca,bc->tba", paley_mixed, sylvester(local_order), precision=lax.Precision.HIGHEST
    )
    local_mixed = local_mixed.reshape(row_count, shard_width)
    factor = 1.0 / math.sqrt(shard_width * tp_count)
    own_start = seq_index * row_count
    own_scale = lax.dynamic_slice_in_dim(token_scale, own_start, row_count)
    combined = local_mixed
    for bit_number in range(tp_count.bit_length() - 1):
        partner = from_partner(combined, "tp", bit_number)
        upper_half = tp_index // (1 << bit_number) % 2
        combined = jnp.where(upper_half == 0, combined + partner, partner - combined)
    quantized = jnp.clip(combined * factor / own_scale[:, None], -127.0, 127.0).astype(jnp.bfloat16)
    column_scale = jnp.exp2(exponents.astype(jnp.float32))
    partial_sums = scaled_product(
        lax.all_gather(quantized, "seq", axis=0, tiled=True),
        weight_codes,
        token_scale,
        column_scale,
    )
    return lax.psum_scatter(partial_sums, "tp", scatter_dimension=0, tiled=True).astype(
        jnp.bfloat16
    )


def solution(mesh):
    placed = (P("seq", "tp"), P("seq", "tp"), P("tp", "seq"), P("seq"), P())
    return jax.shard_map(
        body, mesh=mesh, in_specs=placed, out_specs=P("tp", "seq"), check_vma=False
    )
```

profile of v0, /device:TPU:6, one launch (start us, length us, event | category | flops | bytes accessed | tf_op | source)
XLA Modules:
  0.0 386.7 jit_solution(4026006873668995143)
XLA Ops:
  6.5 0.0 all-gather.2.cloned.1.call-start
  6.5 1.4 fusion.5
  7.9 0.0 copy-start.2
  7.9 0.3 copy.26
  8.2 0.1 reshape.9
  8.3 1.0 fusion.6
  9.3 1.5 convolution_bitcast_fusion
  10.9 0.5 copy.28
  11.4 0.1 reshape.10
  11.5 0.3 copy.30
  11.8 3.8 collective-permute-start
  15.6 0.0 copy-start.5
  15.7 15.4 %collective-permute-done = f32[96,1792]{1,0:T(8,128)S(1)} collective-permute-done((f32[96,1792]{1,0:T(8,128)S(1)}, f32[96,1792]{1,0:T(8,128)S(1)}, u32[]{:S(2)}, u32[]{:S(2)}) %collective-permute-start) | collective-permute-done | bytes 688160 | tf_op jit(solution)/shard_map/ppermute | solution.py:13
  31.0 1.2 subtract_select_fusion.2
  32.2 5.2 %collective-permute-start.1 = (f32[96,1792]{1,0:T(8,128)S(1)}, f32[96,1792]{1,0:T(8,128)S(1)}, u32[]{:S(2)}, u32[]{:S(2)}) collective-permute-start(f32[96,1792]{1,0:T(8,128)S(1)} %subtract_select_fusion.2), channel_id=1, source_target_pairs={{0,2},{1,3},{2,0},{3,1},{4,6},{5,7},{6,4},{7,5},{8,10},{9,11},{10,... | collective-permute-start | bytes 2064392 | tf_op jit(solution)/shard_map/ppermute | solution.py:13
  37.5 0.0 copy-start.4
  37.5 29.5 %collective-permute-done.1 = f32[96,1792]{1,0:T(8,128)S(1)} collective-permute-done((f32[96,1792]{1,0:T(8,128)S(1)}, f32[96,1792]{1,0:T(8,128)S(1)}, u32[]{:S(2)}, u32[]{:S(2)}) %collective-permute-start.1) | collective-permute-done | bytes 688160 | tf_op jit(solution)/shard_map/ppermute | solution.py:13
  66.9 0.1 subtract_select_fusion.1
  67.0 9.1 %collective-permute-start.2 = (f32[96,1792]{1,0:T(8,128)S(1)}, f32[96,1792]{1,0:T(8,128)S(1)}, u32[]{:S(2)}, u32[]{:S(2)}) collective-permute-start(f32[96,1792]{1,0:T(8,128)S(1)} %subtract_select_fusion.1), channel_id=1, source_target_pairs={{0,4},{1,5},{2,6},{3,7},{4,0},{5,1},{6,2},{7,3},{8,12},{9,13},{10,... | collective-permute-start | bytes 2064392 | tf_op jit(solution)/shard_map/ppermute | solution.py:13
  76.1 72.7 %collective-permute-done.2 = f32[96,1792]{1,0:T(8,128)S(1)} collective-permute-done((f32[96,1792]{1,0:T(8,128)S(1)}, f32[96,1792]{1,0:T(8,128)S(1)}, u32[]{:S(2)}, u32[]{:S(2)}) %collective-permute-start.2) | collective-permute-done | bytes 688160 | tf_op jit(solution)/shard_map/ppermute | solution.py:13
  148.8 0.1 subtract_select_fusion
  148.9 42.8 %collective-permute-start.3 = (f32[96,1792]{1,0:T(8,128)S(1)}, f32[96,1792]{1,0:T(8,128)S(1)}, u32[]{:S(2)}, u32[]{:S(2)}) collective-permute-start(f32[96,1792]{1,0:T(8,128)S(1)} %subtract_select_fusion), channel_id=1, source_target_pairs={{0,8},{1,9},{2,10},{3,11},{4,12},{5,13},{6,14},{7,15},{8,0},{9,1},... | collective-permute-start | bytes 2064392 | tf_op jit(solution)/shard_map/ppermute | solution.py:13
  191.7 0.1 dynamic_slice.3
  191.8 30.3 %collective-permute-done.3 = f32[96,1792]{1,0:T(8,128)S(1)} collective-permute-done((f32[96,1792]{1,0:T(8,128)S(1)}, f32[96,1792]{1,0:T(8,128)S(1)}, u32[]{:S(2)}, u32[]{:S(2)}) %collective-permute-start.3) | collective-permute-done | bytes 688160 | tf_op jit(solution)/shard_map/ppermute | solution.py:13
  222.1 0.9 clamp_convert_fusion
  223.0 0.0 all-gather.2.cloned.1.call-update
  223.0 0.0 reduce-scatter.2.cloned.1.call-start
  223.1 69.6 %all-gather.2.cloned.1.call-done = bf16[3072,1792]{1,0:T(8,128)(2,1)} async-done(((bf16[96,1792]{1,0:T(8,128)(2,1)}), bf16[3072,1792]{1,0:T(8,128)(2,1)}) %all-gather.2.cloned.1.call-update) | async-done | bytes 11010064 | tf_op jit(solution)/shard_map/all_gather | solution.py:68
  292.7 8.9 %fusion = f32[3072,256]{1,0:T(8,128)} fusion(bf16[3072,1792]{1,0:T(8,128)(2,1)} %all-gather.2.cloned.1.call-done, bf16[1792,256]{1,0:T(8,128)(2,1)S(1)} %copy-done, f32[256]{0:T(256)S(1)} %multiply_exponential_fusion, f32[3072]{0:T(1024)S(1)} %copy-done.5), kind=kOutput, calls=%fused_computation.1 | convolution fusion | flops 2820145152 | bytes 15086592 | tf_op jit(solution)/shard_map/dot_general | solution.py:39
  301.6 0.0 reduce-scatter.2.cloned.1.call-update
  301.6 76.6 %reduce-scatter.2.cloned.1.call-done = f32[192,256]{1,0:T(8,128)} async-done(((f32[3072,256]{1,0:T(8,128)}), f32[192,256]{1,0:T(8,128)}) %reduce-scatter.2.cloned.1.call-update) | async-done | bytes 196624 | tf_op jit(solution)/shard_map/reduce_scatter | solution.py:73
  378.3 1.6 convert_element_type.19
  (10 shorter events, 0.0 us)
Async XLA Ops:
  6.5 286.2 %copy-start = (bf16[1792,256]{1,0:T(8,128)(2,1)S(1)}, bf16[1792,256]{1,0:T(8,128)(2,1)}, u32[]{:S(2)}) copy-start(bf16[1792,256]{1,0:T(8,128)(2,1)} %param.9) | copy-start | bytes 2752516
  6.5 1.8 copy-start.3
  6.5 286.2 %all-gather.2.cloned.1.call-start = ((), (), s32[]{:S(2)}) async-start(), calls=%async_computation.1 | async-start | bytes 11354112 | tf_op jit(solution)/shard_map/all_gather | solution.py:68
  7.9 1.4 copy-start.2
  11.8 3.9 copy-start.1
  11.8 19.3 %collective-permute-start = (f32[96,1792]{1,0:T(8,128)S(1)}, f32[96,1792]{1,0:T(8,128)S(1)}, u32[]{:S(2)}, u32[]{:S(2)}) collective-permute-start(f32[96,1792]{1,0:T(8,128)S(1)} %copy.30), channel_id=1, source_target_pairs={{0,1},{1,0},{2,3},{3,2},{4,5},{5,4},{6,7},{7,6},{8,9},{9,8},{10,11... | collective-permute-start | bytes 2064392 | tf_op jit(solution)/shard_map/ppermute | solution.py:13
  15.6 176.1 %copy-start.5 = (f32[3072]{0:T(1024)S(1)}, f32[3072]{0:T(1024)}, u32[]{:S(2)}) copy-start(f32[3072]{0:T(1024)} %param.11) | copy-start | bytes 36868
  32.2 34.7 %collective-permute-start.1 = (f32[96,1792]{1,0:T(8,128)S(1)}, f32[96,1792]{1,0:T(8,128)S(1)}, u32[]{:S(2)}, u32[]{:S(2)}) collective-permute-start(f32[96,1792]{1,0:T(8,128)S(1)} %subtract_select_fusion.2), channel_id=1, source_target_pairs={{0,2},{1,3},{2,0},{3,1},{4,6},{5,7},{6,4},{7,5},{8,10},{9,11},{10,... | collective-permute-start | bytes 2064392 | tf_op jit(solution)/shard_map/ppermute | solution.py:13
  37.5 185.6 %copy-start.4 = (s32[256]{0:T(256)S(1)}, s32[256]{0:T(256)}, u32[]{:S(2)}) copy-start(s32[256]{0:T(256)} %param.10) | copy-start | bytes 3076
  67.0 81.8 %collective-permute-start.2 = (f32[96,1792]{1,0:T(8,128)S(1)}, f32[96,1792]{1,0:T(8,128)S(1)}, u32[]{:S(2)}, u32[]{:S(2)}) collective-permute-start(f32[96,1792]{1,0:T(8,128)S(1)} %subtract_select_fusion.1), channel_id=1, source_target_pairs={{0,4},{1,5},{2,6},{3,7},{4,0},{5,1},{6,2},{7,3},{8,12},{9,13},{10,... | collective-permute-start | bytes 2064392 | tf_op jit(solution)/shard_map/ppermute | solution.py:13
  148.9 73.2 %collective-permute-start.3 = (f32[96,1792]{1,0:T(8,128)S(1)}, f32[96,1792]{1,0:T(8,128)S(1)}, u32[]{:S(2)}, u32[]{:S(2)}) collective-permute-start(f32[96,1792]{1,0:T(8,128)S(1)} %subtract_select_fusion), channel_id=1, source_target_pairs={{0,8},{1,9},{2,10},{3,11},{4,12},{5,13},{6,14},{7,15},{8,0},{9,1},... | collective-permute-start | bytes 2064392 | tf_op jit(solution)/shard_map/ppermute | solution.py:13
  223.0 155.3 %reduce-scatter.2.cloned.1.call-start = ((), (), s32[]{:S(2)}) async-start(), calls=%async_computation.2 | async-start | bytes 3342336 | tf_op jit(solution)/shard_map/reduce_scatter | solution.py:73
Sparse Core Ops, SparseCore 0:
  223.1 69.5 all-gather.1
  301.8 76.4 reduce-scatter.1
where the time goes:
time: 387 us
  waiting for transfers between devices  294 us (76%)
  starting transfers between devices  60.9 us (16%)
  between operations  13.7 us (4%)
  matrix products  11.4 us (3%)
  other arithmetic  5.2 us (1%)
    ppermute x4, waiting for transfers between devices, from_partner(): return lax.ppermute(value, axis, pairs)  148 us
    reduce_scatter x1, waiting for transfers between devices, body(): lax.psum_scatter(partial_sums, 'tp', scatter_dimension=0, tiled=True)  76.6 us
    all_gather x1, waiting for transfers between devices, body(): lax.all_gather(quantized, 'seq', axis=0, tiled=True)  69.6 us
    ppermute x4, starting transfers between devices, from_partner(): return lax.ppermute(value, axis, pairs)  60.9 us
    dot_general x1, matrix products, scaled_product(): jnp.dot(row_piece, weight_codes, preferred_element_type=jnp.float32)  8.9 us
  transfers between devices with their start and end apart: 6, of which 6 were waited for; matrix products, arithmetic and copies ran while one was open for 0% of the time, Pallas kernels for 0%

commit v1 on v0

v1 whole, which is shorter than its diff:
```python
import functools, math
import jax, jax.numpy as jnp, numpy as np
from jax import lax
from jax.experimental import pallas as pl
from jax.experimental.pallas import tpu as pltpu
from jax.sharding import PartitionSpec as P
MESH = pl.DeviceIdType.MESH

def paley_table():
    residues = [number * number % 13 for number in range(1, 13)]
    legendre = np.array([0.0] + [1.0 if number in residues else -1.0 for number in range(1, 13)])
    offsets = (np.arange(13)[None, :] - np.arange(13)[:, None]) % 13
    conference = np.zeros((14, 14))
    conference[0, 1:] = 1.0
    conference[1:, 0] = 1.0
    conference[1:, 1:] = legendre[offsets]
    upper_pair = np.array([[1.0, 1.0], [1.0, -1.0]])
    lower_pair = np.array([[1.0, -1.0], [-1.0, -1.0]])
    return np.kron(conference, upper_pair) + np.kron(np.eye(14), lower_pair)

def sylvester(n):
    t = np.ones((1, 1))
    d = np.array([[1.0, 1.0], [1.0, -1.0]])
    for _ in range(n.bit_length() - 1):
        t = np.kron(d, t)
    return t

Z = 16
T = 14
ROWS = 96

def k1(gate_ref, up_ref, scale_ref, mix_ref, out_ref, send_buf, recv_buf, q_buf,
       send1, recv1, send2, recv2):
    z = lax.axis_index("tp")
    core = lax.rem(lax.axis_index("seq"), 2)
    barrier = pltpu.get_barrier_semaphore()
    for d in range(1, Z):
        pl.semaphore_signal(barrier, inc=1, device_id={"tp": lax.rem(z + d, Z)}, device_id_type=MESH)

    g = gate_ref[...].astype(jnp.float32)
    hidden = g / (1.0 + jnp.exp(-g)) * up_ref[...].astype(jnp.float32)
    hi = hidden.astype(jnp.bfloat16)
    lo = (hidden - hi.astype(jnp.float32)).astype(jnp.bfloat16)
    half = T * 128 // 2
    stacked = jnp.concatenate([hi[:, :half], hi[:, half:], lo[:, :half], lo[:, half:]], axis=0)
    mixed = jnp.dot(stacked, mix_ref[...], preferred_element_type=jnp.float32)
    first = mixed[:ROWS] + mixed[2 * ROWS:3 * ROWS]
    second = mixed[ROWS:2 * ROWS] + mixed[3 * ROWS:]
    plus = (first + second).astype(jnp.bfloat16)
    minus = (first - second).astype(jnp.bfloat16)
    for t in range(T // 2):
        send_buf[t] = plus[:, t * 128:(t + 1) * 128]
        send_buf[T // 2 + t] = minus[:, t * 128:(t + 1) * 128]
    pl.semaphore_wait(barrier, Z - 1)

    shift = 8 * core
    mine = lax.rem(z + Z - shift, Z)
    order = [8, 7, 9, 6, 10, 5, 11, 4, 12, 3, 13, 2, 14, 1, 15]

    def copy1(tile, slot, dest):
        return pltpu.make_async_remote_copy(
            src_ref=send_buf.at[tile], dst_ref=recv_buf.at[slot], send_sem=send1.at[tile],
            recv_sem=recv1.at[slot], device_id={"tp": dest}, device_id_type=MESH)

    def copy2(dest, tile):
        return pltpu.make_async_remote_copy(
            src_ref=q_buf.at[dest], dst_ref=out_ref.at[:, pl.ds(pl.multiple_of(tile * 128, 128), 128)],
            send_sem=send2.at[dest], recv_sem=recv2.at[tile], device_id={"tp": dest}, device_id_type=MESH)

    for d in order:
        dest = lax.rem(z + d, Z)
        tile = lax.rem(dest + Z - shift, Z)
        @pl.when(tile < T)
        def _():
            copy1(tile, z, dest).start()

    @pl.when(mine < T)
    def _():
        recv_buf[z] = send_buf[mine]
        for d in order:
            src = lax.rem(z + Z - d, Z)
            copy1(mine, src, src).wait_recv()
        def rows(r, c):
            sl = pl.ds(r * 16, 16)
            v = [recv_buf[i, sl, :].astype(jnp.float32) for i in range(Z)]
            step = 1
            while step < Z:
                nv = list(v)
                for i in range(Z):
                    if i & step == 0:
                        nv[i] = v[i] + v[i | step]
                        nv[i | step] = v[i] - v[i | step]
                v = nv
                step *= 2
            sc = scale_ref[sl, :]
            for i in range(Z):
                q_buf[i, sl, :] = jnp.clip(v[i] * sc, -127.0, 127.0).astype(jnp.bfloat16)
            return c
        lax.fori_loop(0, ROWS // 16, rows, 0)
        for d in order:
            dest = lax.rem(z + d, Z)
            copy2(dest, mine).start()
        out_ref[:, pl.ds(pl.multiple_of(mine * 128, 128), 128)] = q_buf[z]

    for d in order:
        src = lax.rem(z + Z - d, Z)
        tile = lax.rem(src + Z - shift, Z)
        @pl.when(tile < T)
        def _():
            copy2(src, tile).wait_recv()
            copy1(tile, z, src).wait_send()
    @pl.when(mine < T)
    def _():
        for d in order:
            copy2(lax.rem(z + d, Z), mine).wait_send()


def rotate(gate, up, scale):
    mix = jnp.asarray(np.kron(sylvester(32), paley_table()).T, jnp.bfloat16)
    v = pl.BlockSpec(memory_space=pltpu.VMEM)
    dma = pltpu.SemaphoreType.DMA
    buf = pltpu.VMEM((Z, ROWS, 128), jnp.bfloat16)
    return pl.pallas_call(
        k1, out_shape=jax.ShapeDtypeStruct((ROWS, T * 128), jnp.bfloat16),
        in_specs=[v] * 4, out_specs=v,
        scratch_shapes=[buf, buf, buf, dma((Z,)), dma((Z,)), dma((Z,)), dma((Z,))],
        compiler_params=pltpu.CompilerParams(collective_id=0, has_side_effects=True, vmem_limit_bytes=40 << 20),
    )(gate, up, scale, mix)


WIDE = 3

ORDER = [(0, 0), (1, 0), (3, 0), (0, 1), (0, 3), (2, 0), (0, 2), (1, 1), (3, 1), (1, 3), (3, 3),
         (2, 1), (2, 3), (1, 2), (3, 2), (2, 2)]
CLASS = [[0], [1, 2, 3, 4], [5, 6, 7, 8, 9, 10], [11, 12, 13, 14], [15]]


def packed(values):
    word = sum(v << (2 * i) for i, v in enumerate(values))
    return word - (1 << 32) if word >= 1 << 31 else word


def k2(q_ref, w_ref, row_ref, col_ref, out_ref, act, part, in16, in32, st16, st32,
       ag_recv, sib_recv, ag_send, rs_recv, rs_send):
    z = lax.axis_index("tp")
    seq = lax.axis_index("seq")
    core = lax.rem(seq, 2)
    x, y = seq // 8, lax.rem(seq // 2, 4)
    u = x * (1 - core) + y * core
    v = y * (1 - core) + x * core

    def place(uu, vv):
        return 8 * (uu * (1 - core) + vv * core) + 2 * (vv * (1 - core) + uu * core) + core

    def chip(du, dv):
        return place(lax.rem(u + du, 4), lax.rem(v + dv, 4)) // 2

    up_u, dn_u = place(lax.rem(u + 1, 4), v), place(lax.rem(u + 3, 4), v)
    up_v, dn_v = place(u, lax.rem(v + 1, 4)), place(u, lax.rem(v + 3, 4))
    sibling = seq + 1 - 2 * core
    up_z, dn_z = lax.rem(z + 1, Z), lax.rem(z + 15, Z)

    barrier = pltpu.get_barrier_semaphore()
    for peer in (up_u, dn_u, up_v, dn_v, sibling):
        pl.semaphore_signal(barrier, inc=1, device_id={"seq": peer}, device_id_type=MESH)
    for peer in (up_z, dn_z):
        pl.semaphore_signal(barrier, inc=1, device_id={"tp": peer}, device_id_type=MESH)
    for h in range(2):
        act[seq, h] = q_ref[pl.ds(48 * h, 48), :]
    pl.semaphore_wait(barrier, 7)

    def send(block, h, slot, peer):
        return pltpu.make_async_remote_copy(
            src_ref=act.at[block, h], dst_ref=act.at[block, h], send_sem=ag_send.at[block // 2, h, slot],
            recv_sem=ag_recv.at[block // 2, h], device_id={"seq": peer}, device_id_type=MESH)

    def to_sibling(block, h):
        return pltpu.make_async_remote_copy(
            src_ref=act.at[block, h], dst_ref=act.at[block, h], send_sem=ag_send.at[block // 2, h, 4],
            recv_sem=sib_recv.at[block // 2, h], device_id={"seq": sibling}, device_id_type=MESH)

    def rightward(bu, bv, h):
        return lax.rem(bu + bv + h, 2) == 0

    def starts(du, dv, h):
        bu, bv = lax.rem(u + du, 4), lax.rem(v + dv, 4)
        block = place(bu, bv)
        right = rightward(bu, bv, h)
        if dv == 0:
            if du == 0:
                yield send(block, h, 0, up_u), None
                yield send(block, h, 1, dn_u), None
            elif du == 3:
                yield send(block, h, 0, up_u), right
            elif du == 1:
                yield send(block, h, 1, dn_u), jnp.logical_not(right)
            yield send(block, h, 2, up_v), None
            yield send(block, h, 3, dn_v), None
        elif dv == 3:
            yield send(block, h, 2, up_v), right
        elif dv == 1:
            yield send(block, h, 3, dn_v), jnp.logical_not(right)
        yield to_sibling(block, h), None

    def run(du, dv, h, what):
        for copy, cond in starts(du, dv, h):
            if cond is None:
                getattr(copy, what)()
            else:
                pl.when(cond)(getattr(copy, what))

    def receive(classes):
        for h in range(2):
            for s in CLASS[classes]:
                du, dv = ORDER[s]
                block = place(lax.rem(u + du, 4), lax.rem(v + dv, 4))
                send(block, h, 0, seq).wait_recv()
                run(du, dv, h, "start")

    def chain(source, e, k, wide, rows):
        buf = (st32, in32) if wide else (st16, in16)
        return pltpu.make_async_remote_copy(
            src_ref=buf[0].at[k, rows], dst_ref=buf[1].at[e, k, rows], send_sem=rs_send.at[e, k],
            recv_sem=rs_recv.at[e, k], device_id={"tp": jnp.where(e == 0, up_z, dn_z)}, device_id_type=MESH)

    ALL, FIRST, SECOND = pl.ds(0, 192), pl.ds(0, 96), pl.ds(96, 96)

    def distance(k):
        d = lax.rem(k - z + Z, Z)
        e = jnp.where(d > 8, 1, 0)
        return jnp.where(d > 8, Z - d, d), e

    def hop(k, dist, e):
        def add(rows, wide):
            got = in32 if wide else in16
            return part[k, rows, :] + got[e, k, rows, :].astype(jnp.float32)

        @pl.when(dist == 8)
        def _():
            st16[k] = part[k].astype(jnp.bfloat16)
            chain(None, 0, k, False, FIRST).start()
            chain(None, 1, k, False, SECOND).start()

        @pl.when(dist == 7)
        def _():
            held = pl.ds(pl.multiple_of(e * 96, 96), 96)
            own = pl.ds(pl.multiple_of(96 - e * 96, 96), 96)
            chain(None, e, k, False, held).wait_recv()
            st16[k, held, :] = add(held, False).astype(jnp.bfloat16)
            st16[k, own, :] = part[k, own, :].astype(jnp.bfloat16)
            chain(None, e, k, False, ALL).start()

        @pl.when((dist < 7) & (dist > WIDE))
        def _():
            chain(None, e, k, False, ALL).wait_recv()
            st16[k] = add(ALL, False).astype(jnp.bfloat16)
            chain(None, e, k, False, ALL).start()

        @pl.when(dist == WIDE)
        def _():
            chain(None, e, k, False, ALL).wait_recv()
            st32[k] = add(ALL, False)
            chain(None, e, k, True, ALL).start()

        @pl.when((dist < WIDE) & (dist > 0))
        def _():
            chain(None, e, k, True, ALL).wait_recv()
            st32[k] = add(ALL, True)
            chain(None, e, k, True, ALL).start()

        @pl.when(dist == 0)
        def _():
            chain(None, 0, k, True, ALL).wait_recv()
            chain(None, 1, k, True, ALL).wait_recv()
            total = part[k] + in32[0, k] + in32[1, k]
            out_ref[...] = (total * row_ref[...] * col_ref[...]).astype(jnp.bfloat16)

    du_word, dv_word = packed([o[0] for o in ORDER]), packed([o[1] for o in ORDER])

    def chip_at(s):
        du = (du_word >> (2 * s)) & 3
        dv = (dv_word >> (2 * s)) & 3
        return chip(du, dv)

    def hops(s, low, high):
        def one(j, carry):
            k = chip_at(s - j)
            dist, e = distance(k)
            @pl.when(dist == 8 - j)
            def _():
                hop(k, dist, e)
            return carry
        lax.fori_loop(low, high, one, 0)

    def multiply(classes):
        def step(s, carry):
            k = chip_at(s)
            for h in range(2):
                pltpu.make_async_remote_copy(
                    src_ref=act.at[0, 0], dst_ref=act.at[2 * k + 1 - core, h], send_sem=ag_send.at[k, h, 4],
                    recv_sem=sib_recv.at[k, h], device_id={"seq": sibling}, device_id_type=MESH).wait_recv()
            rows = act[pl.ds(2 * k, 2)].reshape(192, 1792)
            part[k] = jnp.dot(rows, w_ref[...], preferred_element_type=jnp.float32)
            hops(s, 0, jnp.minimum(s, 8) + 1)
            return carry
        lax.fori_loop(CLASS[classes][0], CLASS[classes][-1] + 1, step, 0)

    for h in range(2):
        run(0, 0, h, "start")
    receive(1)
    multiply(0)
    receive(2)
    multiply(1)
    receive(3)
    multiply(2)
    receive(4)
    multiply(3)
    multiply(4)

    def drain(s, carry):
        hops(s, s - 15, 9)
        return carry
    lax.fori_loop(16, 24, drain, 0)

    for h in range(2):
        for du, dv in ORDER:
            run(du, dv, h, "wait_send")

    def settle(k, carry):
        dist, e = distance(k)
        @pl.when(dist == 8)
        def _():
            chain(None, 0, k, False, FIRST).wait_send()
            chain(None, 1, k, False, SECOND).wait_send()
        @pl.when((dist < 8) & (dist > WIDE))
        def _():
            chain(None, e, k, False, ALL).wait_send()
        @pl.when((dist <= WIDE) & (dist > 0))
        def _():
            chain(None, e, k, True, ALL).wait_send()
        return carry
    lax.fori_loop(0, Z, settle, 0)


def project(q, w, row_scale, col_scale):
    v = pl.BlockSpec(memory_space=pltpu.VMEM)
    dma = pltpu.SemaphoreType.DMA
    bf, f32 = jnp.bfloat16, jnp.float32
    return pl.pallas_call(
        k2, out_shape=jax.ShapeDtypeStruct((192, 256), bf),
        in_specs=[v] * 4, out_specs=v,
        scratch_shapes=[
            pltpu.VMEM((32, 2, 48, 1792), bf), pltpu.VMEM((16, 192, 256), f32),
            pltpu.VMEM((2, 16, 192, 256), bf), pltpu.VMEM((2, 16, 192, 256), f32),
            pltpu.VMEM((16, 192, 256), bf), pltpu.VMEM((16, 192, 256), f32),
            dma((16, 2)), dma((16, 2)), dma((16, 2, 5)), dma((2, 16)), dma((2, 16))],
        compiler_params=pltpu.CompilerParams(collective_id=1, has_side_effects=True, vmem_limit_bytes=56 << 20),
    )(q, w, row_scale, col_scale)


def body(gate, up, w, exponents, ts):
    own = lax.dynamic_slice_in_dim(ts, lax.axis_index("seq") * ROWS, ROWS)
    scale = jnp.broadcast_to(((1.0 / math.sqrt(28672)) / own)[:, None], (ROWS, 128))
    q = rotate(gate, up, scale)
    row = lax.dynamic_slice_in_dim(ts, lax.axis_index("tp") * 192, 192)[:, None]
    return project(q, w, row, jnp.exp2(exponents.astype(jnp.float32))[None, :])


def solution(mesh):
    placed = (P("seq", "tp"), P("seq", "tp"), P("tp", "seq"), P("seq"), P())
    return jax.shard_map(body, mesh=mesh, in_specs=placed, out_specs=P("tp", "seq"), check_vma=False)
```

time: 387 us -> 181 us (0.47)
  the two profiles are of different devices: /device:TPU:6 before, /device:TPU:68 now
where the time goes in v1:
time: 181 us
  Pallas kernels  171 us (94%)
  local copies, waits for them, and re-layouts  7.25 us (4%)
  other arithmetic  2 us (1%)
    pallas_call x1, Pallas kernels, project(): pl.pallas_call(k2, out_shape=jax.ShapeDtypeStruct((192, 256), bf), in_spe...  124 us
    pallas_call x1, Pallas kernels, rotate(): pl.pallas_call(k1, out_shape=jax.ShapeDtypeStruct((ROWS, T * 128), jnp.bf...  47.7 us
    unnamed x9, local copies, waits for them, and re-layouts  5.62 us

profile of v1, /device:TPU:68, one launch (start us, length us, event | category | flops | bytes accessed | tf_op | source)
XLA Modules:
  0.0 180.6 jit_solution(15195753173452294789)
XLA Ops:
  0.0 0.8 dynamic-slice_divide_fusion
  0.8 0.8 dynamic_slice.7
  1.5 1.2 multiply_exponential_fusion
  2.8 0.1 broadcast_in_dim.12.scale_ref
  2.9 0.8 copy.7.row_ref
  3.6 0.0 copy-start
  3.6 1.4 copy-done
  5.0 0.0 copy-start.2
  5.0 1.0 copy-done.2
  6.0 0.0 copy-start.3
  6.0 1.0 copy-done.3
  7.0 47.7 %shard_map.64.q_ref = bf16[96,1792]{1,0:T(8,128)(2,1)S(1)} custom-call(bf16[96,1792]{1,0:T(8,128)(2,1)S(1)} %copy-done.2, bf16[96,1792]{1,0:T(8,128)(2,1)S(1)} %copy-done.3, f32[96,128]{1,0:T(8,128)S(1)} %broadcast_in_dim.12.scale_ref, bf16[896,896]{1,0:T(8,128)(2,1)S(1)} %copy-done), custom_call_target="tpu_custom_call" | custom-call | tf_op jit(solution)/shard_map/pallas_call | solution.py:123
  54.7 0.0 copy-start.1
  54.7 0.7 copy-done.1
  55.4 123.7 %shard_map.65 = bf16[192,256]{1,0:T(8,128)(2,1)} custom-call(bf16[96,1792]{1,0:T(8,128)(2,1)} %copy-done.1, bf16[1792,256]{1,0:T(8,128)(2,1)} %w_ref.1, f32[192,1]{1,0:T(8,128)} %copy.7.row_ref, f32[1,256]{1,0:T(1,128)} %bitcast.2), custom_call_target="tpu_custom_call" | custom-call | tf_op jit(solution)/shard_map/pallas_call | solution.py:349
  179.1 1.5 copy.9
Async XLA Ops:
  3.6 1.4 copy-start
  5.0 1.0 copy-start.2
  6.0 1.0 copy-start.3
  54.7 0.7 copy-start.1

commit v2 on v0

v2 whole, which is shorter than its diff:
```python
import math

import jax
import jax.numpy as jnp
import numpy as np
from jax import lax
from jax.experimental import pallas as pl
from jax.experimental.pallas import tpu as pltpu
from jax.sharding import PartitionSpec as P

MESH = pl.DeviceIdType.MESH
Z = 16
TILES = 14
ROWS = 96
WIDTH = 1792
COLS = 256
SIZES = (16, 16, 16, 16, 16, 16)
OFFS = tuple(sum(SIZES[:i]) for i in range(len(SIZES)))
CHUNKS = len(SIZES)
DIRECT = (False, False, False, False, False, False)
FAR = (8, 7, 9, 6, 10, 5, 11, 4, 12, 3, 13, 2, 14, 1, 15)
TREES = ((0, 2, 0, 2, 2, 6, 0, 6, 6, 11, 11, 0, 11, 14, 0, 14),
         (0, 0, 3, 0, 3, 6, 3, 6, 6, 11, 11, 14, 11, 14, 0, 14),
         (0, 0, 0, 2, 2, 4, 4, 6, 6, 10, 12, 12, 14, 14, 0, 0))
TREE = (0, 0, 0, 0, 0, 0)
BLOCKS = ((1, 0), (3, 0), (2, 0), (0, 1), (0, 3), (1, 1), (1, 3), (3, 1), (3, 3), (2, 1), (2, 3), (0, 2), (1, 2), (3, 2),
          (2, 2))
GROUPS = (0, 1, 3, 2)
SCHED = (
    "R0", "A0", "R1", "A1", "R2", "R3", "R4", "R5", "S0", "A2", "S1", "A3", "G0", "S2", "A4", "E0.2", "G1",
    "E0.0", "E0.1", "E0.3", "E0.4", "S3", "A5", "E0.9", "E0.10", "G2", "E1.2", "E1.0", "E1.1", "E1.3", "E1.4",
    "E0.5", "E0.6", "E0.7", "E0.8", "S4", "E0.11", "M0.01", "E0.14", "E2.2", "G3", "E2.0", "E2.1", "E2.3",
    "E2.4", "E1.9", "E1.10", "E1.5", "E1.6", "E1.7", "S5", "E0.12", "E0.13", "E1.8", "E1.11", "M0.12", "E2.9",
    "M0.23", "G4", "E2.10", "E3.2", "E3.0", "E3.1", "M0.34", "E3.3", "E2.5", "E3.4", "E2.6", "M1.01", "E2.7",
    "E2.8", "E2.11", "M2.01", "E1.14", "E1.12", "E1.13", "M1.12", "E2.14", "M1.23", "G5", "E4.2", "E4.0",
    "E4.1", "M1.34", "E4.3", "E3.9", "E4.4", "E3.10", "H0.2", "E3.5", "H0.6", "E3.6", "H0.11", "E3.7", "H0.14",
    "E3.8", "E3.11", "M3.01", "E2.12", "E2.13", "M2.13", "E5.2", "E5.0", "E5.1", "E5.3", "M2.34", "E4.9",
    "E5.4", "E4.10", "H1.2", "E4.5", "H1.6", "E4.6", "E4.7", "H1.11", "E4.8", "H1.14", "E4.11", "M4.01",
    "E3.14", "E3.12", "E3.13", "K0", "M3.12", "E5.9", "E5.10", "E5.5", "E5.6", "M3.23", "E5.7", "E5.8", "E5.11",
    "H2.2", "E4.14", "E4.12", "H2.6", "E4.13", "H2.11", "H2.14", "M3.34", "M4.13", "K1", "E5.14", "M4.34",
    "E5.12", "M5.01", "E5.13", "M5.14", "K2", "H3.2", "H3.6", "H3.11", "H3.14", "H4.2", "H4.6", "H4.11",
    "H4.14", "H5.2", "H5.6", "H5.11", "H5.14", "K3", "K4", "K5",
)


def paley_table():
    residues = [number * number % 13 for number in range(1, 13)]
    legendre = np.array([0.0] + [1.0 if number in residues else -1.0 for number in range(1, 13)])
    offsets = (np.arange(13)[None, :] - np.arange(13)[:, None]) % 13
    conference = np.zeros((14, 14))
    conference[0, 1:] = 1.0
    conference[1:, 0] = 1.0
    conference[1:, 1:] = legendre[offsets]
    upper_pair = np.array([[1.0, 1.0], [1.0, -1.0]])
    lower_pair = np.array([[1.0, -1.0], [-1.0, -1.0]])
    return np.kron(conference, upper_pair) + np.kron(np.eye(14), lower_pair)


def sylvester(order):
    table = np.ones((1, 1))
    doubling = np.array([[1.0, 1.0], [1.0, -1.0]])
    for _ in range(order.bit_length() - 1):
        table = np.kron(doubling, table)
    return table


def kernel(gate_hbm, up_hbm, w_hbm, mix_hbm, ts_ref, exp_ref, out_ref,
           gate, up, w, mix, send_buf, recv_buf, q_buf, act, part, staged, landed, scale_ref,
           in_sem, a1_send, a1_recv, a2_send, a2_recv, ag_send, ag_recv, sib_recv, rs_send, rs_recv):
    f32, bf16 = jnp.float32, jnp.bfloat16
    z = lax.axis_index("tp")
    seq = lax.axis_index("seq")
    core = lax.rem(seq, 2)
    x, y = seq // 8, lax.rem(seq // 2, 4)
    u = x * (1 - core) + y * core
    v = y * (1 - core) + x * core
    sibling = seq + 1 - 2 * core

    def place(uu, vv):
        return 8 * (uu * (1 - core) + vv * core) + 2 * (vv * (1 - core) + uu * core) + core

    def at_u(d):
        return place(lax.rem(u + d, 4), v)

    def at_v(d):
        return place(u, lax.rem(v + d, 4))

    def at_z(d):
        return lax.rem(z + d, Z)

    loads = [pltpu.make_async_copy(src, dst, in_sem.at[i])
             for i, (src, dst) in enumerate(((gate_hbm, gate), (up_hbm, up), (mix_hbm, mix), (w_hbm, w)))]
    for load in loads:
        load.start()

    barrier = pltpu.get_barrier_semaphore()
    for d in FAR:
        pl.semaphore_signal(barrier, inc=1, device_id={"tp": at_z(d)}, device_id_type=MESH)
    for d in (2, 1, 3):
        pl.semaphore_signal(barrier, inc=1, device_id={"seq": at_u(d)}, device_id_type=MESH)
        pl.semaphore_signal(barrier, inc=1, device_id={"seq": at_v(d)}, device_id_type=MESH)
    pl.semaphore_signal(barrier, inc=1, device_id={"seq": sibling}, device_id_type=MESH)

    def column(first, count):
        tokens = lax.broadcasted_iota(jnp.int32, (count, 3072), 1)
        wanted = lax.broadcasted_iota(jnp.int32, (count, 3072), 0) + first
        return jnp.sum(jnp.where(tokens == wanted, ts_ref[...], 0.0), axis=1, keepdims=True)

    scale_ref[...] = jnp.broadcast_to((1.0 / math.sqrt(28672)) / column(ROWS * seq, ROWS), (ROWS, 128))

    def rows_of(i):
        return pl.ds(OFFS[i], SIZES[i])

    def pairs_of(i):
        return pl.ds(2 * OFFS[i], 2 * SIZES[i])

    shift = 8 * core
    mine = lax.rem(z + Z - shift, Z)

    def mix_rows(i):
        n, rows = SIZES[i], rows_of(i)
        g = gate[rows, :].astype(f32)
        hidden = g / (1.0 + jnp.exp(-g)) * up[rows, :].astype(f32)
        hi = hidden.astype(bf16)
        lo = (hidden - hi.astype(f32)).astype(bf16)
        half = WIDTH // 2
        stacked = jnp.concatenate([hi[:, :half], hi[:, half:], lo[:, :half], lo[:, half:]], axis=0)
        mixed = jnp.dot(stacked, mix[...], preferred_element_type=f32)
        first = mixed[:n] + mixed[2 * n:3 * n]
        second = mixed[n:2 * n] + mixed[3 * n:]
        plus = (first + second).astype(bf16)
        minus = (first - second).astype(bf16)
        for t in range(TILES // 2):
            send_buf[t, rows, :] = plus[:, t * 128:(t + 1) * 128]
            send_buf[TILES // 2 + t, rows, :] = minus[:, t * 128:(t + 1) * 128]

    def to_combiner(i, tile, slot, dest):
        return pltpu.make_async_remote_copy(
            src_ref=send_buf.at[tile, rows_of(i)], dst_ref=recv_buf.at[slot, rows_of(i)], send_sem=a1_send.at[i],
            recv_sem=a1_recv.at[i], device_id={"tp": dest}, device_id_type=MESH)

    def send_tiles(i):
        for d in FAR:
            dest = at_z(d)
            tile = lax.rem(dest + Z - shift, Z)
            @pl.when(tile < TILES)
            def _():
                to_combiner(i, tile, z, dest).start()

    def bytes_of(buf, count, rows, send_sem, recv_sem, what):
        copy = pltpu.make_async_remote_copy(
            src_ref=buf.at[pl.ds(0, count), rows], dst_ref=buf.at[pl.ds(0, count), rows], send_sem=send_sem,
            recv_sem=recv_sem, device_id={"tp": at_z(1)}, device_id_type=MESH)
        getattr(copy, what)()

    def from_combiner(i, dest):
        lanes = pl.ds(pl.multiple_of(mine * 128, 128), 128)
        return pltpu.make_async_remote_copy(
            src_ref=q_buf.at[dest, rows_of(i)], dst_ref=act.at[seq, rows_of(i), lanes],
            send_sem=a2_send.at[i], recv_sem=a2_recv.at[i], device_id={"tp": dest}, device_id_type=MESH)

    def combine(i):
        @pl.when(mine < TILES)
        def _():
            recv_buf[z, rows_of(i), :] = send_buf[mine, rows_of(i), :]
            bytes_of(recv_buf, Z - 1, rows_of(i), a1_send.at[i], a1_recv.at[i], "wait_recv")

            def some(r, carry):
                rows = pl.ds(pl.multiple_of(OFFS[i] + r * 16, 16), 16)
                held = [recv_buf[j, rows, :].astype(f32) for j in range(Z)]
                step = 1
                while step < Z:
                    held = [held[j] + held[j | step] if j & step == 0 else held[j ^ step] - held[j]
                            for j in range(Z)]
                    step *= 2
                factor = scale_ref[rows, :]
                for j in range(Z):
                    q_buf[j, rows, :] = jnp.clip(held[j] * factor, -127.0, 127.0).astype(bf16)
                return carry

            lax.fori_loop(0, SIZES[i] // 16, some, 0)
            for d in FAR:
                from_combiner(i, at_z(d)).start()
            act[seq, rows_of(i), pl.ds(pl.multiple_of(mine * 128, 128), 128)] = q_buf[z, rows_of(i), :]

    def along(block, i, peer):
        return pltpu.make_async_remote_copy(
            src_ref=act.at[block, rows_of(i)], dst_ref=act.at[block, rows_of(i)], send_sem=ag_send.at[i],
            recv_sem=ag_recv.at[i, block // 2], device_id={"seq": peer}, device_id_type=MESH)

    def to_sibling(block, i):
        return pltpu.make_async_remote_copy(
            src_ref=act.at[block, rows_of(i)], dst_ref=act.at[block, rows_of(i)], send_sem=ag_send.at[i],
            recv_sem=sib_recv.at[i, block // 8], device_id={"seq": sibling}, device_id_type=MESH)

    def pass_on(i, du, dv):
        bu, bv = lax.rem(u + du, 4), lax.rem(v + dv, 4)
        block = place(bu, bv)
        if dv == 0:
            if du == 0:
                for d in (2, 1, 3):
                    along(block, i, at_u(d)).start()
            for d in ((2, 1, 3) if DIRECT[i] else (1, 3)):
                along(block, i, at_v(d)).start()
        elif dv != 2 and not DIRECT[i]:
            right = lax.rem(bu + bv + i, 2) == 0
            pl.when(right if dv == 3 else jnp.logical_not(right))(along(block, i, at_v(4 - dv)).start)
        to_sibling(block, i).start()


    def gather(i):
        have = mine < TILES
        @pl.when(have)
        def _():
            bytes_of(recv_buf, TILES - 1, rows_of(i), a2_send.at[i], a2_recv.at[i], "wait_recv")
        @pl.when(jnp.logical_not(have))
        def _():
            bytes_of(recv_buf, TILES, rows_of(i), a2_send.at[i], a2_recv.at[i], "wait_recv")
        pass_on(i, 0, 0)

    def receive(i, j):
        du, dv = BLOCKS[j]
        block = place(lax.rem(u + du, 4), lax.rem(v + dv, 4))
        along(block, i, seq).wait_recv()
        pass_on(i, du, dv)

    def children(i, pos):
        return [p for p in range(1, Z) if TREES[TREE[i]][p] == pos]

    def word(values, bits):
        total = sum(value << (bits * j) for j, value in enumerate(values))
        return total - (1 << 32) if total >= 1 << 31 else total

    def parent_of(i, pos):
        tree = TREES[TREE[i]]
        half = jnp.where(pos < 8, word(tree[:8], 4), word(tree[8:], 4))
        return (half >> (4 * lax.rem(pos, 8))) & 15

    def device_at(k, pos):
        return jnp.where(lax.rem(k, 2) == 0, lax.rem(k + pos, Z), lax.rem(k + Z - pos, Z))

    def target_at(pos):
        k = lax.rem(z + Z - pos, Z)
        return jnp.where(lax.rem(k, 2) == 0, k, lax.rem(z + pos, Z))

    def summed(i, pos, kind, dest):
        return pltpu.make_async_remote_copy(
            src_ref=staged.at[pos, pairs_of(i)], dst_ref=landed.at[pos, pairs_of(i)], send_sem=rs_send.at[i],
            recv_sem=rs_recv.at[i, kind], device_id={"tp": dest}, device_id_type=MESH)

    def multiply(i, groups):
        n = SIZES[i]
        def one(g, carry):
            dx = (sum(d << (2 * j) for j, d in enumerate(GROUPS)) >> (2 * g)) & 3
            xx = lax.rem(x + dx, 4)
            bytes_of(act, 4, rows_of(i), ag_send.at[i], sib_recv.at[i, xx], "wait_recv")
            rows = act[pl.ds(8 * xx, 8), rows_of(i), :].reshape(8 * n, WIDTH)
            product = jnp.dot(rows, w[...], preferred_element_type=f32)
            for j in range(4):
                k = 4 * xx + j
                mine_of = product[j * 2 * n:(j + 1) * 2 * n]
                p = lax.rem(z + Z - k, Z)
                pos = jnp.where(lax.rem(k, 2) == 0, p, lax.rem(Z - p, Z))
                parent = parent_of(i, pos)
                part[k, pairs_of(i), :] = mine_of
                staged[pos, pairs_of(i), :] = mine_of.astype(bf16)
                leaves = word([p > 0 and not children(i, p) for p in range(Z)], 1)
                @pl.when(((leaves >> pos) & 1) == 1)
                def _():
                    summed(i, pos, parent, device_at(k, parent)).start()
            return carry
        lax.fori_loop(groups[0], groups[1], one, 0)

    def collect(i, pos):
        below, parent = children(i, pos), TREES[TREE[i]][pos]
        bytes_of(landed, len(below), pairs_of(i), rs_send.at[i], rs_recv.at[i, pos], "wait_recv")
        k = target_at(pos)
        total = part[k, pairs_of(i), :]
        for child in below:
            total = total + landed[child, pairs_of(i), :].astype(f32)
        staged[pos, pairs_of(i), :] = total.astype(bf16)
        summed(i, pos, parent, device_at(k, parent)).start()

    def finish(i):
        n = SIZES[i]
        below = children(i, 0)
        bytes_of(landed, len(below), pairs_of(i), rs_send.at[i], rs_recv.at[i, 0], "wait_recv")
        total = part[z, pairs_of(i), :]
        for pos in below:
            total = total + landed[pos, pairs_of(i), :].astype(f32)
        total = total * columns
        for c in range(2):
            rows = column(192 * z + ROWS * c + OFFS[i], n)
            out_ref[pl.ds(ROWS * c + OFFS[i], n), :] = (total[c * n:(c + 1) * n] * rows).astype(bf16)

    columns = jnp.exp2(exp_ref[...].astype(f32))
    started, weights = False, False
    for task in SCHED:
        name, i = task[0], int(task[1])
        rest = int(task[3:] or 0)
        if name == "R":
            if not started:
                for load in loads[:3]:
                    load.wait()
            mix_rows(i)
            if not started:
                pl.semaphore_wait(barrier, Z - 1 + 3 + 3 + 1)
            started = True
        elif name == "A":
            send_tiles(i)
        elif name == "S":
            combine(i)
        elif name == "G":
            gather(i)
        elif name == "E":
            receive(i, rest)
        elif name == "M":
            if not weights:
                loads[3].wait()
            weights = True
            multiply(i, (rest // 10, rest % 10))
        elif name == "H":
            collect(i, rest)
        elif name == "K":
            finish(i)

    for i in range(CHUNKS):
        bytes_of(act, 31, rows_of(i), ag_send.at[i], ag_recv.at[i, 0], "wait_send")
        bytes_of(staged, 15, pairs_of(i), rs_send.at[i], rs_recv.at[i, 0], "wait_send")
        @pl.when(mine < TILES)
        def _():
            bytes_of(send_buf, TILES - 1, rows_of(i), a1_send.at[i], a1_recv.at[i], "wait_send")
            bytes_of(recv_buf, Z - 1, rows_of(i), a2_send.at[i], a2_recv.at[i], "wait_send")
        @pl.when(mine >= TILES)
        def _():
            bytes_of(send_buf, TILES, rows_of(i), a1_send.at[i], a1_recv.at[i], "wait_send")


def body(gate, up, weight_codes, exponents, token_scale):
    bf16, f32 = jnp.bfloat16, jnp.float32
    mix = jnp.asarray(np.kron(sylvester(32), paley_table()).T, bf16)
    vmem, hbm = pl.BlockSpec(memory_space=pltpu.VMEM), pl.BlockSpec(memory_space=pl.ANY)
    dma = pltpu.SemaphoreType.DMA
    tiles = pltpu.VMEM((Z, ROWS, 128), bf16)
    return pl.pallas_call(
        kernel,
        out_shape=jax.ShapeDtypeStruct((2 * ROWS, COLS), bf16),
        in_specs=[hbm] * 4 + [vmem] * 2,
        out_specs=vmem,
        scratch_shapes=[
            pltpu.VMEM((ROWS, WIDTH), bf16), pltpu.VMEM((ROWS, WIDTH), bf16), pltpu.VMEM((WIDTH, COLS), bf16),
            pltpu.VMEM((WIDTH // 2, WIDTH // 2), bf16), tiles, tiles, tiles,
            pltpu.VMEM((32, ROWS, WIDTH), bf16), pltpu.VMEM((Z, 2 * ROWS, COLS), f32),
            pltpu.VMEM((Z, 2 * ROWS, COLS), bf16), pltpu.VMEM((Z, 2 * ROWS, COLS), bf16),
            pltpu.VMEM((ROWS, 128), f32),
            dma((4,)), dma((CHUNKS,)), dma((CHUNKS,)), dma((CHUNKS,)), dma((CHUNKS,)),
            dma((CHUNKS,)), dma((CHUNKS, 16)), dma((CHUNKS, 4)), dma((CHUNKS,)), dma((CHUNKS, Z))],
        compiler_params=pltpu.CompilerParams(collective_id=0, has_side_effects=True, vmem_limit_bytes=56 << 20),
    )(gate, up, weight_codes, mix, token_scale.reshape(1, -1), exponents.reshape(1, -1))


def solution(mesh):
    placed = (P("seq", "tp"), P("seq", "tp"), P("tp", "seq"), P("seq"), P())
    return jax.shard_map(
        body, mesh=mesh, in_specs=placed, out_specs=P("tp", "seq"), check_vma=False
    )
```

time: 387 us -> 93.9 us (0.24)
  waiting for transfers between devices: 294 us -> 0 us
  Pallas kernels: 0 us -> 90.7 us
  starting transfers between devices: 60.9 us -> 0 us
  between operations: 13.7 us -> 0.01 us
  matrix products: 11.4 us -> 0 us
  other arithmetic: 5.2 us -> 0 us
    ppermute x4 -> x0, waiting for transfers between devices: 148 us -> none  [from_partner(): return lax.ppermute(value, axis, pairs)]
    pallas_call x0 -> x1, Pallas kernels: none -> 90.7 us  [body(): pl.pallas_call(kernel, out_shape=jax.ShapeDtypeStruct((2 * ROWS, COLS), b...]
    reduce_scatter x1 -> x0, waiting for transfers between devices: 76.6 us -> none  [body(): lax.psum_scatter(partial_sums, 'tp', scatter_dimension=0, tiled=True)]
    all_gather x1 -> x0, waiting for transfers between devices: 69.6 us -> none  [body(): lax.all_gather(quantized, 'seq', axis=0, tiled=True)]
    ppermute x4 -> x0, starting transfers between devices: 60.9 us -> none  [from_partner(): return lax.ppermute(value, axis, pairs)]
    dot_general x3 -> x0, matrix products: 11.4 us -> none  [the longest x1 8.9 us: scaled_product(): jnp.dot(row_piece, weight_codes, preferred_element_type=jnp.float32)]
  transfers between devices with their start and end apart: 6 -> 0, of which waited for: 6 -> 0; matrix products, arithmetic and copies ran while one was open for 0% -> 0% of each run, Pallas kernels for 0% -> 0%
where the time goes in v2:
time: 93.9 us; the launch traced here: 92.2 us
  Pallas kernels  90.7 us (97%)
  local copies, waits for them, and re-layouts  1.54 us (2%)
    pallas_call x1, Pallas kernels, body(): pl.pallas_call(kernel, out_shape=jax.ShapeDtypeStruct((2 * ROWS, COLS), b...  90.7 us

profile of v2, /device:TPU:6, one launch (start us, length us, event | category | flops | bytes accessed | tf_op | source)
XLA Modules:
  0.0 92.2 jit_solution(2874090261446433416)
XLA Ops:
  0.0 90.7 %shard_map.64 = bf16[192,256]{1,0:T(8,128)(2,1)} custom-call(bf16[96,1792]{1,0:T(8,128)(2,1)} %gate_hbm.1, bf16[96,1792]{1,0:T(8,128)(2,1)} %up_hbm.1, bf16[1792,256]{1,0:T(8,128)(2,1)} %w_hbm.1, bf16[896,896]{1,0:T(8,128)(2,1)} %constant.2.clone.mix_hbm, f32[1,3072]{1,0:T(1,128)} %bitcast.2, s32[1,256]{1,0:T(1,128)} %bitcast.3), custom_call_target="tpu_custom_call" | custom-call | tf_op jit(solution)/shard_map/pallas_call | solution.py:345
  90.7 1.5 %copy.8 = bf16[192,256]{1,0:T(8,128)(2,1)} copy(bf16[192,256]{1,0:T(8,128)(2,1)} %shard_map.64) | data formatting | bytes 196608

commit v3 on v2

--- a/solution.py
+++ b/solution.py
@@ -27,19 +27,19 @@
           (2, 2))
 GROUPS = (0, 1, 3, 2)
 SCHED = (
-    "R0", "A0", "R1", "A1", "R2", "R3", "R4", "R5", "S0", "A2", "S1", "A3", "G0", "S2", "A4", "E0.2", "G1",
-    "E0.0", "E0.1", "E0.3", "E0.4", "S3", "A5", "E0.9", "E0.10", "G2", "E1.2", "E1.0", "E1.1", "E1.3", "E1.4",
-    "E0.5", "E0.6", "E0.7", "E0.8", "S4", "E0.11", "M0.01", "E0.14", "E2.2", "G3", "E2.0", "E2.1", "E2.3",
-    "E2.4", "E1.9", "E1.10", "E1.5", "E1.6", "E1.7", "S5", "E0.12", "E0.13", "E1.8", "E1.11", "M0.12", "E2.9",
-    "M0.23", "G4", "E2.10", "E3.2", "E3.0", "E3.1", "M0.34", "E3.3", "E2.5", "E3.4", "E2.6", "M1.01", "E2.7",
-    "E2.8", "E2.11", "M2.01", "E1.14", "E1.12", "E1.13", "M1.12", "E2.14", "M1.23", "G5", "E4.2", "E4.0",
-    "E4.1", "M1.34", "E4.3", "E3.9", "E4.4", "E3.10", "H0.2", "E3.5", "H0.6", "E3.6", "H0.11", "E3.7", "H0.14",
-    "E3.8", "E3.11", "M3.01", "E2.12", "E2.13", "M2.13", "E5.2", "E5.0", "E5.1", "E5.3", "M2.34", "E4.9",
-    "E5.4", "E4.10", "H1.2", "E4.5", "H1.6", "E4.6", "E4.7", "H1.11", "E4.8", "H1.14", "E4.11", "M4.01",
-    "E3.14", "E3.12", "E3.13", "K0", "M3.12", "E5.9", "E5.10", "E5.5", "E5.6", "M3.23", "E5.7", "E5.8", "E5.11",
-    "H2.2", "E4.14", "E4.12", "H2.6", "E4.13", "H2.11", "H2.14", "M3.34", "M4.13", "K1", "E5.14", "M4.34",
-    "E5.12", "M5.01", "E5.13", "M5.14", "K2", "H3.2", "H3.6", "H3.11", "H3.14", "H4.2", "H4.6", "H4.11",
-    "H4.14", "H5.2", "H5.6", "H5.11", "H5.14", "K3", "K4", "K5",
+    "R0", "A0", "R1", "A1", "R2", "R3", "R4", "R5", "S0", "A2", "S1", "A3", "G0", "S2", "A4", "G1", "E0.2",
+    "E0.0", "E0.1", "E0.3", "E0.4", "S3", "A5", "E1.2", "G2", "E1.0", "E1.1", "E1.3", "E1.4", "E0.9", "E0.10",
+    "E0.5", "E0.6", "E0.7", "S4", "E0.8", "E0.11", "M0.01", "G3", "E1.9", "E1.10", "E2.2", "E2.0", "E2.1",
+    "E2.3", "E2.4", "S5", "E1.5", "E1.6", "E1.7", "E1.8", "E1.11", "M1.01", "E0.14", "E0.12", "E0.13", "M0.13",
+    "G4", "E3.2", "E3.0", "E3.1", "E3.3", "M0.34", "E1.14", "E3.4", "E2.9", "E2.10", "E2.5", "E2.6", "E2.7",
+    "E2.8", "E2.11", "M2.01", "E1.12", "E1.13", "M1.13", "G5", "E4.2", "M1.34", "E4.0", "E4.1", "E4.3", "E4.4",
+    "E3.9", "H0.2", "E3.10", "H0.6", "E3.5", "H0.11", "E3.6", "H0.14", "E3.7", "E3.8", "E3.11", "M3.01",
+    "E2.14", "E2.12", "E2.13", "M2.13", "E5.2", "E5.0", "E5.1", "M2.34", "E5.3", "E4.9", "E5.4", "E4.10",
+    "H1.2", "E4.5", "H1.6", "E4.6", "H1.11", "E4.7", "E4.8", "H1.14", "E4.11", "M4.01", "E3.14", "E3.12",
+    "E3.13", "M3.12", "K0", "M3.23", "E5.9", "E5.10", "E5.5", "M3.34", "E5.6", "E5.7", "E5.8", "H2.2", "E5.11",
+    "H2.6", "E4.14", "E4.12", "H2.11", "H2.14", "E4.13", "M4.13", "M5.01", "K1", "M4.34", "E5.14", "E5.12",
+    "M5.12", "E5.13", "H3.2", "H3.6", "H3.11", "H3.14", "M5.24", "K2", "H4.2", "H4.6", "H4.11", "H4.14", "K3",
+    "H5.2", "H5.6", "H5.11", "H5.14", "K4", "K5",
 )
 
 

time: 93.9 us -> 94.1 us (level); the launches traced: 92.2 us -> 93.5 us
  Pallas kernels: 90.7 us -> 91.9 us
    pallas_call x1, Pallas kernels: 90.7 us -> 91.9 us  [body(): pl.pallas_call(kernel, out_shape=jax.ShapeDtypeStruct((2 * ROWS, COLS), b...]
where the time goes in v3:
time: 94.1 us; the launch traced here: 93.5 us
  Pallas kernels  91.9 us (98%)
  local copies, waits for them, and re-layouts  1.54 us (2%)
    pallas_call x1, Pallas kernels, body(): pl.pallas_call(kernel, out_shape=jax.ShapeDtypeStruct((2 * ROWS, COLS), b...  91.9 us

profile of v3, /device:TPU:6, one launch (start us, length us, event | category | flops | bytes accessed | tf_op | source)
XLA Modules:
  0.0 93.5 jit_solution(566739699132453174)
XLA Ops:
  0.0 91.9 %shard_map.64 = bf16[192,256]{1,0:T(8,128)(2,1)} custom-call(bf16[96,1792]{1,0:T(8,128)(2,1)} %gate_hbm.1, bf16[96,1792]{1,0:T(8,128)(2,1)} %up_hbm.1, bf16[1792,256]{1,0:T(8,128)(2,1)} %w_hbm.1, bf16[896,896]{1,0:T(8,128)(2,1)} %constant.2.clone.mix_hbm, f32[1,3072]{1,0:T(1,128)} %bitcast.2, s32[1,256]{1,0:T(1,128)} %bitcast.3), custom_call_target="tpu_custom_call" | custom-call | tf_op jit(solution)/shard_map/pallas_call | solution.py:345
  91.9 1.5 %copy.8 = bf16[192,256]{1,0:T(8,128)(2,1)} copy(bf16[192,256]{1,0:T(8,128)(2,1)} %shard_map.64) | data formatting | bytes 196608
